TPU v7x, 128 devices: a whole 4x4x4 slice. The times are simulated.
128 devices in a mesh: row: 8 (over x, core), col: 16 (over y, z).
Axes of the slice: x: 4, y: 4, z: 4, core: 2. Of those that a mesh axis runs over, the one named last changes fastest.
Arguments:
- a_tiles: bfloat16 [8, 16, 3, 8, 128, 128], P('row', 'col'), may hold values from -0.15625 to 0.15625
- a_rows: int32 [8, 16, 3, 8], P('row'), may hold values from 0 to 15, as said below
- a_cols: int32 [8, 16, 3, 8], P('row'), may hold values from 0 to 15, as said below
- p_tiles: bfloat16 [8, 3, 2, 16, 4, 128, 128], P('row', None, None, 'col'), may hold values from -6 to 6
- p_cols: int32 [8, 3, 2, 16, 4], P(None, None, None, 'col'), may hold values from 0 to 7, as said below
- owners: int32 [128, 1], P('row'), may hold values from 0 to 15; in each aligned block of 16 rows (0 to 15, 16 to 31, ...) at most 2 rows name the same one
Outputs:
- owned_rows: bfloat16 [256, 128, 128, 128], P(('row', 'col'))
Inputs may be any that keep to these rules, and one draw needn't show every extreme that they name: For each row group and panel, the pairs (a_rows, a_cols) over all columns of devices and all 8 slots are distinct. `a_cols`: see a_rows. `p_cols`: the 4 entries of one tile row within one column group are distinct. `owners`: within each row group of 16 tile rows, no owner holds more than 2 of them.
All inputs are finite; a program needn't handle non-finite values.
Results may differ from a plain program's by a relative error of at most 0.001.
Values may be sent and summed in bfloat16 or wider, within the bound.
A program may use at most 128 MiB of HBM per device.

v0:
```python
import jax
import jax.numpy as jnp
from jax import lax
from jax.sharding import PartitionSpec as P

SECTIONS = 3
BC = 8
PJ = 4
MOST = 2


def dense_panel(panel, panel_cols):
    k_count = panel.shape[0]
    tile_size = panel.shape[-1]
    col_ids = jnp.arange(BC, dtype=jnp.int32)
    col_hits = (panel_cols[:, :, None] == col_ids[None, None, :]).astype(jnp.bfloat16)
    placed = jnp.einsum("kjc,kjbd->kbcd", col_hits, panel, preferred_element_type=jnp.float32)
    return placed.astype(jnp.bfloat16).reshape(k_count * tile_size, BC * tile_size)


def make_fold(rows_s, kblk_s, block_rows, k_count):
    row_ids = jnp.arange(block_rows, dtype=jnp.int32)
    k_ids = jnp.arange(k_count, dtype=jnp.int32)

    def fold(carried, piece, start):
        row_hits = (rows_s[:, None] == row_ids[None, :]).astype(jnp.bfloat16)
        k_hits = (kblk_s[:, None] == k_ids[None, :]).astype(jnp.bfloat16)
        places = row_hits[:, :, None] * k_hits[:, None, :]
        placed = jnp.einsum("nrk,nab->rakb", places, piece, preferred_element_type=jnp.float32)
        return placed.astype(jnp.bfloat16)

    return fold


def body(a_tiles, a_rows, a_cols, p_tiles, p_cols, owners):
    col_count = lax.axis_size("col")
    block_rows = owners.shape[0]
    tile_size = a_tiles.shape[-1]
    product = jnp.zeros((block_rows * tile_size, BC * tile_size), jnp.float32)
    for section_idx in range(SECTIONS):
        panel = lax.all_gather(p_tiles[0, section_idx, :, 0], "row", axis=0, tiled=True)
        k_count = panel.shape[0]
        panel_cols = p_cols[:, section_idx, :, 0].reshape(k_count, PJ)
        p_dense = dense_panel(panel, panel_cols)
        rows_s = a_rows[0, :, section_idx].reshape(-1)
        kblk_s = a_cols[0, :, section_idx].reshape(-1)
        fold = make_fold(rows_s, kblk_s, block_rows, k_count)
        empty = jnp.zeros((block_rows, tile_size, k_count, tile_size), jnp.bfloat16)
        a_dense = fold(
            empty,
            lax.all_gather(a_tiles[0, 0, section_idx], "col", axis=0, tiled=True),
            jnp.int32(0),
        )
        a_matrix = a_dense.reshape(block_rows * tile_size, k_count * tile_size)
        product = product + jnp.dot(a_matrix, p_dense, preferred_element_type=jnp.float32)
    rounded = product.astype(jnp.bfloat16).reshape(block_rows, tile_size, BC, tile_size)
    rounded = jnp.transpose(rounded, (0, 2, 1, 3)).reshape(block_rows, BC * tile_size * tile_size)
    owner_list = owners[:, 0]
    index_line = jnp.arange(block_rows, dtype=jnp.int32)
    same_owner = owner_list[:, None] == owner_list[None, :]
    earlier = index_line[None, :] < index_line[:, None]
    rank_line = jnp.sum((same_owner & earlier).astype(jnp.int32), axis=1)
    owner_ids = jnp.arange(col_count, dtype=jnp.int32)
    slot_ids = jnp.arange(MOST, dtype=jnp.int32)
    selector = (rank_line[None, None, :] == slot_ids[:, None, None]) & (
        owner_list[None, None, :] == owner_ids[None, :, None]
    )
    selected = jnp.einsum(
        "qor,rx->qox", selector.astype(jnp.bfloat16), rounded, preferred_element_type=jnp.float32
    )
    outgoing = selected.astype(jnp.bfloat16).reshape(MOST, col_count, BC, tile_size, tile_size)
    incoming = lax.all_to_all(outgoing, "col", split_axis=1, concat_axis=1, tiled=True)
    return incoming.reshape(MOST, col_count * BC, tile_size, tile_size)


def solution(mesh):
    placed = (
        P("row", "col", None, None, None, None),
        P("row", None, None, None),
        P("row", None, None, None),
        P("row", None, None, "col", None, None, None),
        P(None, None, None, "col", None),
        P("row", None),
    )
    return jax.shard_map(
        body,
        mesh=mesh,
        in_specs=placed,
        out_specs=P(("row", "col"), None, None, None),
        check_vma=False,
    )
```

profile of v0, /device:TPU:32, one launch (start us, length us, event | category | flops | bytes accessed | tf_op | source)
XLA Modules:
  0.0 442.6 jit_solution(8993594745007393638)
XLA Ops:
  6.5 0.0 all-gather.19.cloned.1.call-start
  6.6 2.0 slice_bitcast_fusion.2
  8.6 0.0 all-gather.19.cloned.1.call-update
  8.6 0.0 all-gather.23.cloned.1.call-start
  8.7 0.7 all-gather.23.cloned.1.call-update
  9.4 0.0 all-gather.15.cloned.1.call-start
  9.4 0.7 all-gather.15.cloned.1.call-update
  10.1 0.0 all-gather.17.cloned.1.call-start
  10.2 1.2 fusion.60
  11.3 0.9 copy.88
  12.2 0.0 all-gather.17.cloned.1.call-update
  12.2 0.0 all-gather.21.cloned.1.call-start
  12.3 0.9 copy.90
  13.2 0.0 all-gather.21.cloned.1.call-update
  13.2 0.0 all-gather.13.cloned.1.call-start
  13.2 0.9 copy.86
  14.1 0.0 all-gather.13.cloned.1.call-update
  14.2 0.0 copy-done.6
  14.2 0.2 convert_reduce_fusion
  14.4 0.0 copy-done.3
  14.4 0.1 copy.65
  14.5 0.1 eq.229
  14.5 0.0 copy-done.4
  14.6 0.1 copy.66
  14.6 0.1 eq.233
  14.7 0.0 copy-done.5
  14.8 0.1 copy.68
  14.8 0.1 copy.71
  14.9 0.1 eq.241
  15.0 0.1 copy.72
  15.1 0.1 eq.245
  15.2 0.1 copy.74
  15.3 0.1 copy.59
  15.3 0.1 eq.217
  15.4 0.1 copy.60
  15.5 0.1 eq.221
  15.6 0.1 copy.62
  15.7 20.5 %all-gather.19.cloned.1.call-done = bf16[1,1,16,1,4,128,128]{6,5,4,3,1,0,2:T(8,128)(2,1)} async-done(((bf16[1,1,2,1,4,128,128]{6,5,4,3,1,0,2:T(8,128)(2,1)}), bf16[1,1,16,1,4,128,128]{6,5,4,3,1,0,2:T(8,128)(2,1)}) %all-gather.19.cloned.1.call-update) | async-done | bytes 2097168 | tf_op jit(solution)/shard_map/all_gather | solution.py:41
  36.3 5.3 %convolution_convert_fusion.5 = bf16[16,8,128,128]{3,1,2,0:T(8,128)(2,1)} fusion(bf16[1,1,16,1,4,128,128]{6,5,4,3,1,0,2:T(8,128)(2,1)} %all-gather.19.cloned.1.call-done, s32[16,4]{1,0:T(8,128)S(1)} %bitcast.153), kind=kOutput, calls=%fused_computation.26 | convolution fusion | flops 18874880 | bytes 6291712 | tf_op jit(solution)/shard_map/kjc,kjbd->kbcd/dot_general | solution.py:17
  41.5 21.9 %all-gather.23.cloned.1.call-done = bf16[1,1,16,1,4,128,128]{6,5,4,3,1,0,2:T(8,128)(2,1)} async-done(((bf16[1,1,2,1,4,128,128]{6,5,4,3,1,0,2:T(8,128)(2,1)}), bf16[1,1,16,1,4,128,128]{6,5,4,3,1,0,2:T(8,128)(2,1)}) %all-gather.23.cloned.1.call-update) | async-done | bytes 2097168 | tf_op jit(solution)/shard_map/all_gather | solution.py:41
  63.5 5.4 %convolution_convert_fusion.4 = bf16[16,8,128,128]{3,1,2,0:T(8,128)(2,1)} fusion(bf16[1,1,16,1,4,128,128]{6,5,4,3,1,0,2:T(8,128)(2,1)} %all-gather.23.cloned.1.call-done, s32[16,4]{1,0:T(8,128)S(1)} %bitcast.154), kind=kOutput, calls=%fused_computation.25 | convolution fusion | flops 18874880 | bytes 6291712 | tf_op jit(solution)/shard_map/kjc,kjbd->kbcd/dot_general | solution.py:17
  68.8 21.8 %all-gather.15.cloned.1.call-done = bf16[1,1,16,1,4,128,128]{6,5,4,3,1,0,2:T(8,128)(2,1)} async-done(((bf16[1,1,2,1,4,128,128]{6,5,4,3,1,0,2:T(8,128)(2,1)}), bf16[1,1,16,1,4,128,128]{6,5,4,3,1,0,2:T(8,128)(2,1)}) %all-gather.15.cloned.1.call-update) | async-done | bytes 2097168 | tf_op jit(solution)/shard_map/all_gather | solution.py:41
  90.6 5.3 %convolution_convert_fusion.6 = bf16[16,8,128,128]{3,1,2,0:T(8,128)(2,1)} fusion(bf16[1,1,16,1,4,128,128]{6,5,4,3,1,0,2:T(8,128)(2,1)} %all-gather.15.cloned.1.call-done, s32[16,4]{1,0:T(8,128)S(1)} %bitcast.155), kind=kOutput, calls=%fused_computation.27 | convolution fusion | flops 18874880 | bytes 6291712 | tf_op jit(solution)/shard_map/kjc,kjbd->kbcd/dot_general | solution.py:17
  95.9 54.3 %all-gather.17.cloned.1.call-done = bf16[1,1,1,128,128,128]{5,3,4,2,1,0:T(8,128)(2,1)} async-done(((bf16[1,1,1,8,128,128]{5,3,4,2,1,0:T(8,128)(2,1)}), bf16[1,1,1,128,128,128]{5,3,4,2,1,0:T(8,128)(2,1)}) %all-gather.17.cloned.1.call-update) | async-done | bytes 4194320 | tf_op jit(solution)/shard_map/all_gather | solution.py:51
  150.3 7.9 %convolution_convert_fusion.2 = bf16[16,16,128,128]{3,1,2,0:T(8,128)(2,1)} fusion(bf16[1,1,1,128,128,128]{5,3,4,2,1,0:T(8,128)(2,1)} %all-gather.17.cloned.1.call-done, bf16[128,16]{0,1:T(8,128)(2,1)S(1)} %get-tuple-element.23, bf16[128,16]{0,1:T(8,128)(2,1)S(1)} %get-tuple-element.22), kind=kOutput, calls=%fused_computation.12 | convolution fusion | flops 1078067200 | bytes 12591104 | tf_op jit(solution)/shard_map/nrk,nab->rakb/dot_general | solution.py:29
  158.2 51.0 %all-gather.21.cloned.1.call-done = bf16[1,1,1,128,128,128]{5,3,4,2,1,0:T(8,128)(2,1)} async-done(((bf16[1,1,1,8,128,128]{5,3,4,2,1,0:T(8,128)(2,1)}), bf16[1,1,1,128,128,128]{5,3,4,2,1,0:T(8,128)(2,1)}) %all-gather.21.cloned.1.call-update) | async-done | bytes 4194320 | tf_op jit(solution)/shard_map/all_gather | solution.py:51
  209.2 4.7 %convolution_convert_fusion.1 = bf16[16,16,128,128]{3,1,2,0:T(8,128)(2,1)S(1)} fusion(bf16[1,1,1,128,128,128]{5,3,4,2,1,0:T(8,128)(2,1)} %all-gather.21.cloned.1.call-done, bf16[128,16]{0,1:T(8,128)(2,1)S(1)} %get-tuple-element.21, bf16[128,16]{0,1:T(8,128)(2,1)S(1)} %get-tuple-element.20), kind=kOutput, calls=%fused_computation.11 | convolution fusion | flops 1078067200 | bytes 12591104 | tf_op jit(solution)/shard_map/nrk,nab->rakb/dot_general | solution.py:29
  213.9 0.0 copy-done
  213.9 1.1 copy-done.1
  215.1 11.2 %fusion.3 = f32[2048,1024]{1,0:T(8,128)} fusion(bf16[256,8,16,128]{3,2,1,0:T(8,128)(2,1)S(1)} %bitcast.146, bf16[256,8,8,128]{3,2,1,0:T(8,128)(2,1)S(1)} %bitcast.151), kind=kOutput, calls=%fused_computation.4 | convolution fusion | flops 8589934592 | bytes 20971520 | tf_op jit(solution)/shard_map/dot_general | solution.py:55
  226.3 0.0 copy-done.2
  226.3 11.2 %fusion = f32[2048,1024]{1,0:T(8,128)} fusion(bf16[256,8,16,128]{3,2,1,0:T(8,128)(2,1)S(1)} %bitcast.147, bf16[256,8,8,128]{3,2,1,0:T(8,128)(2,1)S(1)} %bitcast.152), kind=kOutput, calls=%fused_computation.1 | convolution fusion | flops 8589934592 | bytes 20971520 | tf_op jit(solution)/shard_map/dot_general | solution.py:55
  237.4 30.8 %all-gather.13.cloned.1.call-done = bf16[1,1,1,128,128,128]{5,3,4,2,1,0:T(8,128)(2,1)} async-done(((bf16[1,1,1,8,128,128]{5,3,4,2,1,0:T(8,128)(2,1)}), bf16[1,1,1,128,128,128]{5,3,4,2,1,0:T(8,128)(2,1)}) %all-gather.13.cloned.1.call-update) | async-done | bytes 4194320 | tf_op jit(solution)/shard_map/all_gather | solution.py:51
  268.2 4.5 %convolution_convert_fusion.3 = bf16[16,16,128,128]{3,1,2,0:T(8,128)(2,1)S(1)} fusion(bf16[1,1,1,128,128,128]{5,3,4,2,1,0:T(8,128)(2,1)} %all-gather.13.cloned.1.call-done, bf16[128,16]{0,1:T(8,128)(2,1)S(1)} %get-tuple-element.25, bf16[128,16]{0,1:T(8,128)(2,1)S(1)} %get-tuple-element.24), kind=kOutput, calls=%fused_computation.13 | convolution fusion | flops 1078067200 | bytes 12591104 | tf_op jit(solution)/shard_map/nrk,nab->rakb/dot_general | solution.py:29
  272.7 14.5 %fusion.9 = bf16[256,8,8,128]{3,1,2,0:T(8,128)(2,1)} fusion(f32[2048,1024]{1,0:T(8,128)} %fusion, f32[2048,1024]{1,0:T(8,128)} %fusion.3, bf16[256,8,8,128]{3,2,1,0:T(8,128)(2,1)} %bitcast.150, bf16[256,8,16,128]{3,2,1,0:T(8,128)(2,1)S(1)} %bitcast.148), kind=kOutput, calls=%fused_computation.14 | convolution fusion | flops 8596226048 | bytes 33554432 | tf_op jit(solution)/shard_map/dot_general | solution.py:55
  287.2 3.3 copy.98
  290.5 0.4 bitcast_bitcast_fusion
  290.9 3.3 copy.77
  294.2 4.7 %reshape.246 = bf16[16,131072,1]{1,0,2:T(8,128)(2,1)} reshape(bf16[16,8,128,128]{3,2,1,0:T(8,128)(2,1)} %copy.77) | data formatting | bytes 8388608 | tf_op jit(solution)/shard_map/reshape | solution.py:57
  298.8 7.9 %convolution_convert_fusion = bf16[2,16,131072]{2,1,0:T(8,128)(2,1)} fusion(bf16[16,131072,1]{1,0,2:T(8,128)(2,1)} %reshape.246, pred[16,16]{1,0:T(8,128)(4,1)S(1)} %iota_compare_fusion.9, pred[2,16]{1,0:T(4,128)(4,1)S(1)} %iota_compare_fusion.11), kind=kOutput, calls=%fused_computation | convolution fusion | flops 138412544 | bytes 12583200 | tf_op jit(solution)/shard_map/qor,rx->qox/dot_general | solution.py:68
  306.7 8.6 %copy.99 = bf16[4,8,1024,128]{3,2,1,0:T(8,128)(2,1)} copy(bf16[4,8,1024,128]{3,1,2,0:T(8,128)(2,1)} %bitcast.144) | data formatting | bytes 16777216
  315.4 10.5 %copy.78 = bf16[2,16,8,128,128]{4,3,2,0,1:T(8,128)(2,1)} copy(bf16[2,16,8,128,128]{4,3,2,1,0:T(8,128)(2,1)} %bitcast.145) | data formatting | bytes 16777216 | tf_op jit(solution)/shard_map/reshape | solution.py:71
  325.9 99.3 %all_to_all.5 = bf16[2,16,8,128,128]{4,3,2,0,1:T(8,128)(2,1)} all-to-all(bf16[2,16,8,128,128]{4,3,2,0,1:T(8,128)(2,1)} %copy.78), channel_id=1, replica_groups=mesh['row'=8,'col'=16] {'col'}, dimensions={1} | all-to-all | bytes 16777216 | tf_op jit(solution)/shard_map/all_to_all | solution.py:72
  425.2 10.5 %copy.79 = bf16[2,16,8,128,128]{4,3,2,1,0:T(8,128)(2,1)} copy(bf16[2,16,8,128,128]{4,3,2,0,1:T(8,128)(2,1)} %all_to_all.5) | data formatting | bytes 16777216 | tf_op jit(solution)/shard_map/all_to_all | solution.py:72
  (15 shorter events, 0.1 us)
Async XLA Ops:
  6.5 7.6 %copy-start.6 = (s32[16,1]{0,1:T(1,128)S(1)}, s32[16,1]{0,1:T(1,128)}, u32[]{:S(2)}) copy-start(s32[16,1]{0,1:T(1,128)} %param.11) | copy-start | bytes 196
  6.5 7.8 %copy-start.3 = (s32[1,16,3,8]{1,3,2,0:T(8,128)S(1)}, s32[1,16,3,8]{1,3,2,0:T(8,128)}, u32[]{:S(2)}) copy-start(s32[1,16,3,8]{1,3,2,0:T(8,128)} %param.7) | copy-start | bytes 4612
  6.5 8.0 %copy-start.4 = (s32[1,16,3,8]{1,3,2,0:T(8,128)S(1)}, s32[1,16,3,8]{1,3,2,0:T(8,128)}, u32[]{:S(2)}) copy-start(s32[1,16,3,8]{1,3,2,0:T(8,128)} %param.8) | copy-start | bytes 4612
  6.5 8.2 %copy-start.5 = (s32[8,3,2,1,4]{0,4,3,2,1:T(4,128)S(1)}, s32[8,3,2,1,4]{0,4,3,2,1:T(4,128)}, u32[]{:S(2)}) copy-start(s32[8,3,2,1,4]{0,4,3,2,1:T(4,128)} %param.10) | copy-start | bytes 2308
  6.5 29.7 %all-gather.19.cloned.1.call-start = ((), (), s32[]{:S(2)}) async-start(), calls=%async_computation.4 | async-start | bytes 2359296 | tf_op jit(solution)/shard_map/all_gather | solution.py:41
  8.6 54.8 %all-gather.23.cloned.1.call-start = ((), (), s32[]{:S(2)}) async-start(), calls=%async_computation.6 | async-start | bytes 2359296 | tf_op jit(solution)/shard_map/all_gather | solution.py:41
  9.4 81.3 %all-gather.15.cloned.1.call-start = ((), (), s32[]{:S(2)}) async-start(), calls=%async_computation.2 | async-start | bytes 2359296 | tf_op jit(solution)/shard_map/all_gather | solution.py:41
  10.1 140.2 %all-gather.17.cloned.1.call-start = ((), (), s32[]{:S(2)}) async-start(), calls=%async_computation.3 | async-start | bytes 4456448 | tf_op jit(solution)/shard_map/all_gather | solution.py:51
  12.2 197.0 %all-gather.21.cloned.1.call-start = ((), (), s32[]{:S(2)}) async-start(), calls=%async_computation.5 | async-start | bytes 4456448 | tf_op jit(solution)/shard_map/all_gather | solution.py:51
  13.2 255.0 %all-gather.13.cloned.1.call-start = ((), (), s32[]{:S(2)}) async-start(), calls=%async_computation.1 | async-start | bytes 4456448 | tf_op jit(solution)/shard_map/all_gather | solution.py:51
  209.2 4.7 %copy-start = (bf16[16,16,128,128]{3,1,2,0:T(8,128)(2,1)S(1)}, bf16[16,16,128,128]{3,1,2,0:T(8,128)(2,1)}, u32[]{:S(2)}) copy-start(bf16[16,16,128,128]{3,1,2,0:T(8,128)(2,1)} %convolution_convert_fusion.2) | copy-start | bytes 25165828
  209.2 5.8 %copy-start.1 = (bf16[16,8,128,128]{3,1,2,0:T(8,128)(2,1)S(1)}, bf16[16,8,128,128]{3,1,2,0:T(8,128)(2,1)}, u32[]{:S(2)}) copy-start(bf16[16,8,128,128]{3,1,2,0:T(8,128)(2,1)} %convolution_convert_fusion.5) | copy-start | bytes 12582916
  215.1 11.2 %copy-start.2 = (bf16[16,8,128,128]{3,1,2,0:T(8,128)(2,1)S(1)}, bf16[16,8,128,128]{3,1,2,0:T(8,128)(2,1)}, u32[]{:S(2)}) copy-start(bf16[16,8,128,128]{3,1,2,0:T(8,128)(2,1)} %convolution_convert_fusion.4) | copy-start | bytes 12582916
Sparse Core Ops, SparseCore 0:
  9.1 27.1 all-gather.18
  38.0 25.4 all-gather.22
  65.2 25.4 all-gather.14
  92.6 57.6 all-gather.16
  152.2 56.9 all-gather.20
  211.2 56.9 all-gather.12
where the time goes:
time: 445 us; the launch traced here: 443 us
  waiting for transfers between devices  202 us (45%)
  blocking collectives  99.3 us (22%)
  matrix products  77.8 us (17%)
  local copies, waits for them, and re-layouts  49.5 us (11%)
  between operations  13.6 us (3%)
    all_gather x3, waiting for transfers between devices, body(): lax.all_gather(a_tiles[0, 0, section_idx], 'col', axis=0, tiled=True)  136 us
    all_to_all x1, blocking collectives, body(): lax.all_to_all(outgoing, 'col', split_axis=1, concat_axis=1, tiled=True)  99.3 us
    all_gather x3, waiting for transfers between devices, body(): lax.all_gather(p_tiles[0, section_idx, :, 0], 'row', axis=0, tiled=True)  64.3 us
    dot_general x3, matrix products, body(): jnp.dot(a_matrix, p_dense, preferred_element_type=jnp.float32)  36.8 us
    unnamed x20, local copies, waits for them, and re-layouts  17.8 us
    dot_general x3, matrix products, fold(): jnp.einsum('nrk,nab->rakb', places, piece, preferred_element_type=jnp.flo...  17.1 us
    dot_general x3, matrix products, dense_panel(): jnp.einsum('kjc,kjbd->kbcd', col_hits, panel, preferred_element_type=jnp....  15.9 us
    all_to_all x1, local copies, waits for them, and re-layouts, body(): lax.all_to_all(outgoing, 'col', split_axis=1, concat_axis=1, tiled=True)  10.5 us
  transfers between devices with their start and end apart: 6, of which 6 were waited for; matrix products, arithmetic and copies ran while one was open for 13% of the time, Pallas kernels for 0%

commit v1 on v0

v1 whole, which is shorter than its diff:
```python
import functools

import jax
import jax.numpy as jnp
from jax import lax
from jax.experimental import pallas as pl
from jax.experimental.pallas import tpu as pltpu
from jax.sharding import PartitionSpec as P

SECTIONS = 3
BR = 16
BK = 16
BC = 8
KA = 8
PJ = 4
MOST = 2
TILE = 128
N_COL = 16
RING = 4
MESH = pl.DeviceIdType.MESH
A_SLOTS = N_COL * KA
P_SLOTS = BK * PJ
P_BASE = SECTIONS * BR * BK
O_BASE = P_BASE + SECTIONS * BK * BC
WIDE = 2
CHUNKS = BC // WIDE
MB = 512

ORDER = (
    (0, 1), (1, 0), (2, 2), (0, 3), (3, 0), (1, 1), (3, 3), (2, 0),
    (0, 2), (1, 3), (3, 1), (1, 2), (2, 1), (3, 2), (2, 3),
)
N_COPIES = SECTIONS * (44 + 7) + CHUNKS * 15


def kernel(tbl, a_ref, p_ref, out_ref, ar0, ar1, ar2, pr0, pr1, pr2, a_dense, p_dense, acc, rounded, staged, ssem, rsem, lsem):
    a_raw, p_raw = (ar0, ar1, ar2), (pr0, pr1, pr2)
    row, col = lax.axis_index("row"), lax.axis_index("col")
    x, core = row // 2, row % 2
    y, z = col // RING, col % RING

    def yz(dy, dz):
        return ((y + dy) % RING) * RING + (z + dz) % RING

    def xc(dx, dc):
        return ((x + dx) % RING) * 2 + (core + dc) % 2

    for s in range(SECTIONS):
        a_raw[s][A_SLOTS] = jnp.zeros((TILE, TILE), jnp.bfloat16)
        p_raw[s][P_SLOTS] = jnp.zeros((TILE, TILE), jnp.bfloat16)
    rounded[BR] = jnp.zeros((WIDE, TILE, TILE), jnp.bfloat16)

    barrier = pltpu.get_barrier_semaphore()
    peers = [{"col": yz(dy, dz)} for dy, dz in ORDER]
    peers += [{"row": xc(dx, 0)} for dx in (1, 3, 2)] + [{"row": xc(0, 1)}]
    for peer in peers:
        pl.semaphore_signal(barrier, inc=1, device_id=peer, device_id_type=MESH)
    pl.semaphore_wait(barrier, len(peers))

    copies = []
    local = []

    def send(src, dst, peer):
        i = len(copies)
        copy = pltpu.make_async_remote_copy(
            src_ref=src, dst_ref=dst, send_sem=ssem.at[i], recv_sem=rsem.at[i], device_id=peer, device_id_type=MESH
        )
        copy.start()
        copies.append(copy)
        return copy

    def keep(src, dst):
        copy = pltpu.make_async_copy(src, dst, lsem.at[len(local)])
        copy.start()
        local.append(copy)
        return copy

    def a_part(s, dy, dz, lo, n):
        return a_raw[s].at[pl.ds(yz(dy, dz) * KA + lo, n)]

    def fwd_a(s, dy, dz, lo, n, ty, tz):
        part = a_part(s, dy, dz, lo, n)
        return send(part, part, {"col": yz(ty, tz)})

    half = KA // 2
    quarter = KA // 4
    got = {}

    def pos(first, d1, d2):
        return (d2, d1) if first == 0 else (d1, d2)

    def stage_own(s):
        for n1 in (1, 3):
            for first in (0, 1):
                for along in (0, 1):
                    to = pos(first, n1, 0) if along == 0 else pos(first, 0, n1)
                    lo = first * half
                    got[s, first, "own", along, n1] = send(
                        a_ref.at[s, pl.ds(lo, half)], a_part(s, 0, 0, lo, half), {"col": yz(*to)}
                    )
        got[s, "kept"] = keep(a_ref.at[s], a_part(s, 0, 0, 0, KA))

    def stage_near(s):
        for n1 in (1, 3):
            for first in (0, 1):
                got[s, first, "own", 0, n1].wait_recv()
                dy, dz = pos(first, -n1, 0)
                lo = first * half
                q = lo + (0 if n1 == 1 else quarter)
                got[s, first, "far", n1] = fwd_a(s, dy, dz, q, quarter, *pos(first, n1, 0))
                for n2 in (1, 3):
                    got[s, first, "turn", n1, n2] = fwd_a(s, dy, dz, lo, half, *pos(first, 0, n2))

    def stage_far(s):
        for n1 in (1, 3):
            for first in (0, 1):
                got[s, first, "far", n1].wait_recv()
                dy, dz = pos(first, 2, 0)
                q = first * half + (0 if n1 == 1 else quarter)
                for n2 in (1, 3):
                    got[s, first, "farturn", n1, n2] = fwd_a(s, dy, dz, q, quarter, *pos(first, 0, n2))

    def stage_second(s, part):
        for n2 in (1, 3):
            for first in (0, 1):
                q = first * half + (0 if n2 == 1 else quarter)
                if part == 0:
                    got[s, first, "own", 1, n2].wait_recv()
                    dy, dz = pos(first, 0, -n2)
                    got[s, first, "end", 0, n2] = fwd_a(s, dy, dz, q, quarter, *pos(first, 0, n2))
                elif part == 1:
                    for n1 in (1, 3):
                        got[s, first, "turn", n1, n2].wait_recv()
                        dy, dz = pos(first, -n1, -n2)
                        got[s, first, "end", n1, n2] = fwd_a(s, dy, dz, q, quarter, *pos(first, 0, n2))
                else:
                    for n1 in (1, 3):
                        got[s, first, "farturn", n1, n2].wait_recv()
                        if n1 == n2:
                            dy, dz = pos(first, 2, -n2)
                            got[s, first, "end", 2, n2] = fwd_a(s, dy, dz, q, quarter, *pos(first, 0, n2))

    def stage_end(s):
        for n2 in (1, 3):
            for first in (0, 1):
                for n1 in (0, 1, 3, 2):
                    got[s, first, "end", n1, n2].wait_recv()
        got[s, "kept"].wait()

    def p_part(s, dx, dc):
        return p_raw[s].at[pl.ds(xc(dx, dc) * 2 * PJ, 2 * PJ)]

    def p_own(s):
        for dx in (1, 3, 2):
            got[s, "p", dx] = send(p_ref.at[s], p_part(s, 0, 0), {"row": xc(dx, 0)})
        got[s, "p", 0] = send(p_ref.at[s], p_part(s, 0, 0), {"row": xc(0, 1)})
        got[s, "pkept"] = keep(p_ref.at[s], p_part(s, 0, 0))

    def p_share(s):
        for dx in (1, 3, 2):
            got[s, "p", dx].wait_recv()
            got[s, "ps", dx] = send(p_part(s, -dx, 0), p_part(s, -dx, 0), {"row": xc(0, 1)})

    def p_end(s):
        got[s, "p", 0].wait_recv()
        for dx in (1, 3, 2):
            got[s, "ps", dx].wait_recv()
        got[s, "pkept"].wait()

    def place_p(s):
        @pl.loop(0, BK)
        def _(k):
            for c in range(BC):
                p_dense[pl.ds(pl.multiple_of(k * TILE, TILE), TILE), c * TILE : (c + 1) * TILE] = p_raw[s][
                    tbl[P_BASE + s * BK * BC + k * BC + c]
                ]

    def place_a(s):
        @pl.loop(0, BR)
        def _(r):
            for k in range(BK):
                a_dense[pl.ds(pl.multiple_of(r * TILE, TILE), TILE), k * TILE : (k + 1) * TILE] = a_raw[s][
                    tbl[s * BR * BK + r * BK + k]
                ]

    def part_dot(mb, nb):
        rows = pl.ds(pl.multiple_of(mb * MB, MB), MB)
        return jnp.dot(
            a_dense[rows, :], p_dense[:, nb * WIDE * TILE : (nb + 1) * WIDE * TILE], preferred_element_type=jnp.float32
        )

    def dots(s, nb):
        @pl.loop(0, BR * TILE // MB)
        def _(mb):
            rows = pl.ds(pl.multiple_of(mb * MB, MB), MB)
            value = part_dot(mb, nb)
            if s == 0:
                acc[nb, rows, :] = value
            else:
                acc[nb, rows, :] += value

    def finish(nb):
        @pl.loop(0, BR * TILE // MB)
        def _(mb):
            rows = pl.ds(pl.multiple_of(mb * MB, MB), MB)
            value = (acc[nb, rows, :] + part_dot(mb, nb)).astype(jnp.bfloat16)
            for i in range(MB // TILE):
                for j in range(WIDE):
                    rounded[mb * (MB // TILE) + i, j] = value[i * TILE : (i + 1) * TILE, j * TILE : (j + 1) * TILE]

        @pl.loop(0, N_COL)
        def _(o):
            for q in range(MOST):
                staged[nb, o, q] = rounded[tbl[O_BASE + o * MOST + q]]

        where = out_ref.at[:, pl.ds(col * BC + nb * WIDE, WIDE)]
        for dy, dz in ORDER:
            got["out", nb, dy, dz] = send(staged.at[nb, yz(dy, dz)], where, {"col": yz(dy, dz)})
        keep(staged.at[nb, col], where)

    stage_own(0)
    p_own(0)
    stage_own(1)
    stage_near(0)
    stage_far(0)
    stage_second(0, 0)
    p_own(1)
    p_own(2)
    stage_second(0, 1)
    stage_second(0, 2)
    stage_own(2)
    stage_near(1)
    p_share(0)
    stage_far(1)
    stage_end(0)
    p_end(0)
    place_p(0)
    place_a(0)
    stage_second(1, 0)
    dots(0, 0)
    stage_second(1, 1)
    dots(0, 1)
    stage_second(1, 2)
    stage_near(2)
    dots(0, 2)
    p_share(1)
    stage_far(2)
    dots(0, 3)
    stage_end(1)
    p_share(2)
    p_end(1)
    stage_second(2, 0)
    place_p(1)
    place_a(1)
    stage_second(2, 1)
    dots(1, 0)
    dots(1, 1)
    stage_second(2, 2)
    dots(1, 2)
    dots(1, 3)
    p_end(2)
    place_p(2)
    stage_end(2)
    place_a(2)
    for nb in range(CHUNKS):
        finish(nb)
    for nb in range(CHUNKS):
        for dy, dz in ORDER:
            got["out", nb, dy, dz].wait_recv()
    for copy in copies:
        copy.wait_send()
    for copy in local[2 * SECTIONS :]:
        copy.wait()


def tables(a_rows, a_cols, p_cols, owners):
    codes = jnp.transpose(a_rows[0] * BK + a_cols[0], (1, 0, 2)).reshape(SECTIONS, A_SLOTS)
    spots = jnp.arange(BR * BK, dtype=jnp.int32)
    slots = jnp.arange(A_SLOTS, dtype=jnp.int32)
    a_tbl = jnp.min(jnp.where(codes[:, None, :] == spots[None, :, None], slots[None, None, :], A_SLOTS), axis=2)
    cols = jnp.transpose(p_cols[:, :, :, 0], (1, 0, 2, 3)).reshape(SECTIONS, P_SLOTS)
    group = jnp.arange(BK * BC, dtype=jnp.int32)
    slots = jnp.arange(P_SLOTS, dtype=jnp.int32)
    place = (slots // PJ)[None, :] * BC + cols
    p_tbl = jnp.min(jnp.where(place[:, None, :] == group[None, :, None], slots[None, None, :], P_SLOTS), axis=2)
    owner = owners[:, 0]
    line = jnp.arange(BR, dtype=jnp.int32)
    rank = jnp.sum(((owner[:, None] == owner[None, :]) & (line[None, :] < line[:, None])).astype(jnp.int32), axis=1)
    spot = owner * MOST + rank
    outs = jnp.arange(N_COL * MOST, dtype=jnp.int32)
    o_tbl = jnp.min(jnp.where(spot[None, :] == outs[:, None], line[None, :], BR), axis=1)
    return jnp.concatenate([a_tbl.reshape(-1), p_tbl.reshape(-1), o_tbl]).astype(jnp.int32)


def body(a_tiles, a_rows, a_cols, p_tiles, p_cols, owners):
    tbl = tables(a_rows, a_cols, p_cols, owners)
    a = a_tiles.reshape(SECTIONS, KA, TILE, TILE)
    p = p_tiles.reshape(SECTIONS, 2 * PJ, TILE, TILE)
    bf = jnp.bfloat16
    return pl.pallas_call(
        kernel,
        name="block_product",
        out_shape=jax.ShapeDtypeStruct((MOST, N_COL * BC, TILE, TILE), bf),
        in_specs=[
            pl.BlockSpec(memory_space=pltpu.SMEM),
            pl.BlockSpec(memory_space=pl.ANY),
            pl.BlockSpec(memory_space=pl.ANY),
        ],
        out_specs=pl.BlockSpec(memory_space=pl.ANY),
        scratch_shapes=[pltpu.VMEM((A_SLOTS + 1, TILE, TILE), bf)] * SECTIONS
        + [pltpu.VMEM((P_SLOTS + 1, TILE, TILE), bf)] * SECTIONS
        + [
            pltpu.VMEM((BR * TILE, BK * TILE), bf),
            pltpu.VMEM((BK * TILE, BC * TILE), bf),
            pltpu.VMEM((CHUNKS, BR * TILE, WIDE * TILE), jnp.float32),
            pltpu.VMEM((BR + 1, WIDE, TILE, TILE), bf),
            pltpu.VMEM((CHUNKS, N_COL, MOST, WIDE, TILE, TILE), bf),
            pltpu.SemaphoreType.DMA((N_COPIES,)),
            pltpu.SemaphoreType.DMA((N_COPIES,)),
            pltpu.SemaphoreType.DMA((2 * SECTIONS + CHUNKS,)),
        ],
        compiler_params=pltpu.CompilerParams(collective_id=0, has_side_effects=True, vmem_limit_bytes=60 << 20),
        cost_estimate=pl.CostEstimate(flops=25_769_803_776, bytes_accessed=20_000_000, transcendentals=0),
    )(tbl, a, p)


def solution(mesh):
    placed = (
        P("row", "col", None, None, None, None),
        P("row", None, None, None),
        P("row", None, None, None),
        P("row", None, None, "col", None, None, None),
        P(None, None, None, "col", None),
        P("row", None),
    )
    return jax.shard_map(
        body,
        mesh=mesh,
        in_specs=placed,
        out_specs=P(("row", "col"), None, None, None),
        check_vma=False,
    )
```

time: 445 us -> 209 us (0.47)
  waiting for transfers between devices: 202 us -> 0 us
  Pallas kernels: 0 us -> 193 us
  blocking collectives: 99.3 us -> 0 us
  matrix products: 77.8 us -> 0 us
  local copies, waits for them, and re-layouts: 49.5 us -> 11.6 us
  between operations: 13.6 us -> 0.03 us
    all_gather x6 -> x0, waiting for transfers between devices: 200 us -> none  [the longest x3 136 us: body(): lax.all_gather(a_tiles[0, 0, section_idx], 'col', axis=0, tiled=True)]
    pallas_call x0 -> x1, Pallas kernels: none -> 193 us  [body(): pl.pallas_call(kernel, name='block_product', out_shape=jax.ShapeDtypeStru...]
    all_to_all x1 -> x0, blocking collectives: 99.3 us -> none  [body(): lax.all_to_all(outgoing, 'col', split_axis=1, concat_axis=1, tiled=True)]
    dot_general x10 -> x0, matrix products: 77.8 us -> none  [the longest x3 36.8 us: body(): jnp.dot(a_matrix, p_dense, preferred_element_type=jnp.float32)]
    reshape x2, local copies, waits for them, and re-layouts: 15.2 us -> 0.11 us  [the longest x1 0.1 us: tables(): jnp.transpose(p_cols[:, :, :, 0], (1, 0, 2, 3)).reshape(SECTIONS, P_SLOTS)]
    all_to_all x1 -> x0, local copies, waits for them, and re-layouts: 10.5 us -> none  [body(): lax.all_to_all(outgoing, 'col', split_axis=1, concat_axis=1, tiled=True)]
    unnamed x20 -> x1, local copies, waits for them, and re-layouts: 17.8 us -> 10.5 us
  transfers between devices with their start and end apart: 6 -> 0, of which waited for: 6 -> 0; matrix products, arithmetic and copies ran while one was open for 13% -> 0% of each run, Pallas kernels for 0% -> 0%
where the time goes in v1:
time: 209 us; the launch traced here: 208 us
  Pallas kernels  193 us (92%)
  local copies, waits for them, and re-layouts  11.6 us (6%)
  other arithmetic  3.31 us (2%)
    pallas_call x1, Pallas kernels, body(): pl.pallas_call(kernel, name='block_product', out_shape=jax.ShapeDtypeStru...  193 us
    unnamed x1, local copies, waits for them, and re-layouts  10.5 us

profile of v1, /device:TPU:32, one launch (start us, length us, event | category | flops | bytes accessed | tf_op | source)
XLA Modules:
  0.0 208.3 jit_solution(15781326318683645434)
XLA Ops:
  0.0 0.9 convert_reduce_fusion
  0.9 0.7 multiply_add_fusion
  1.6 0.1 select_reduce_fusion.2
  1.7 0.7 add_bitcast_fusion
  2.4 0.1 copy.9
  2.5 0.1 eq.26
  2.6 0.2 select_reduce_fusion
  2.8 0.8 copy.10
  3.6 0.1 reshape.60
  3.7 0.1 select_reduce_fusion.1
  3.8 0.6 pad_add_fusion.tbl
  4.4 193.4 %block_product.1 = bf16[2,128,128,128]{3,2,1,0:T(8,128)(2,1)} custom-call(s32[1184]{0:T(1024)} %pad_add_fusion.tbl, bf16[3,8,128,128]{3,2,1,0:T(8,128)(2,1)} %bitcast.14, bf16[3,8,128,128]{3,2,1,0:T(8,128)(2,1)} %bitcast.15), custom_call_target="tpu_custom_call" | custom-call | flops 25769803776 | bytes 20000000 | tf_op jit(solution)/shard_map/block_product/pallas_call | solution.py:300
  197.8 10.5 %copy.12 = bf16[2,128,128,128]{3,2,1,0:T(8,128)(2,1)} copy(bf16[2,128,128,128]{3,2,1,0:T(8,128)(2,1)} %block_product.1) | data formatting | bytes 16777216
  (3 shorter events, 0.0 us)

commit v2 on v1

--- a/solution.py
+++ b/solution.py
@@ -20,11 +20,10 @@
 MESH = pl.DeviceIdType.MESH
 A_SLOTS = N_COL * KA
 P_SLOTS = BK * PJ
-P_BASE = SECTIONS * BR * BK
-O_BASE = P_BASE + SECTIONS * BK * BC
 WIDE = 2
 CHUNKS = BC // WIDE
 MB = 512
+PIECES = 4
 
 ORDER = (
     (0, 1), (1, 0), (2, 2), (0, 3), (3, 0), (1, 1), (3, 3), (2, 0),
@@ -33,7 +32,10 @@
 N_COPIES = SECTIONS * (44 + 7) + CHUNKS * 15
 
 
-def kernel(tbl, a_ref, p_ref, out_ref, ar0, ar1, ar2, pr0, pr1, pr2, a_dense, p_dense, acc, rounded, staged, ssem, rsem, lsem):
+def kernel(
+    a_rows, a_cols, p_cols, owners, a_ref, p_ref, out_ref,
+    ar0, ar1, ar2, pr0, pr1, pr2, a_dense, p_dense, acc, rounded, staged, found, tbl, ssem, rsem, lsem, tsem,
+):
     a_raw, p_raw = (ar0, ar1, ar2), (pr0, pr1, pr2)
     row, col = lax.axis_index("row"), lax.axis_index("col")
     x, core = row // 2, row % 2
@@ -167,12 +169,51 @@
             got[s, "ps", dx].wait_recv()
         got[s, "pkept"].wait()
 
+    def find():
+        def iota(shape, dim):
+            return lax.broadcasted_iota(jnp.int32, shape, dim)
+
+        def column(line):
+            n = line.shape[1]
+            return jnp.sum(jnp.where(iota((n, n), 0) == iota((n, n), 1), line, 0), axis=1, keepdims=True)
+
+        spots = iota((N_COL, BR * BK), 1)
+        first = iota((N_COL, BR * BK), 0) * KA
+        for s in range(SECTIONS):
+            codes = a_rows[s] * BK + a_cols[s]
+            best = jnp.full((N_COL, BR * BK), A_SLOTS, jnp.int32)
+            for t in range(KA):
+                best = jnp.minimum(best, jnp.where(column(codes[t : t + 1]) == spots, first + t, A_SLOTS))
+            found[s : s + 1, :] = jnp.min(best, axis=0, keepdims=True)
+        n_row = BK // 2
+        spots = iota((n_row, BK * BC), 1)
+        group = iota((n_row, BK * BC), 0)
+        for s in range(SECTIONS):
+            best = jnp.full((n_row, BK * BC), P_SLOTS, jnp.int32)
+            for m in range(2):
+                cols = p_cols[s, m]
+                k = group * 2 + m
+                for j in range(PJ):
+                    best = jnp.minimum(best, jnp.where(k * BC + column(cols[j : j + 1]) == spots, k * PJ + j, P_SLOTS))
+            found[SECTIONS + s : SECTIONS + s + 1, : BK * BC] = jnp.min(best, axis=0, keepdims=True)
+        line = iota((BR, TILE), 0)
+        spots = iota((BR, TILE), 1)
+        named = column(owners[...]) == spots // MOST
+        low = jnp.min(jnp.where(named, line, BR), axis=0, keepdims=True)
+        high = jnp.max(jnp.where(named, line, -1), axis=0, keepdims=True)
+        second = jnp.where(high > low, high, BR)
+        slot = iota((1, TILE), 1) % MOST
+        found[2 * SECTIONS : 2 * SECTIONS + 1, :TILE] = jnp.where(slot == 0, low, second)
+        copy = pltpu.make_async_copy(found, tbl, tsem)
+        copy.start()
+        copy.wait()
+
     def place_p(s):
         @pl.loop(0, BK)
         def _(k):
             for c in range(BC):
                 p_dense[pl.ds(pl.multiple_of(k * TILE, TILE), TILE), c * TILE : (c + 1) * TILE] = p_raw[s][
-                    tbl[P_BASE + s * BK * BC + k * BC + c]
+                    tbl[SECTIONS + s, k * BC + c]
                 ]
 
     def place_a(s):
@@ -180,7 +221,7 @@
         def _(r):
             for k in range(BK):
                 a_dense[pl.ds(pl.multiple_of(r * TILE, TILE), TILE), k * TILE : (k + 1) * TILE] = a_raw[s][
-                    tbl[s * BR * BK + r * BK + k]
+                    tbl[s, r * BK + k]
                 ]
 
     def part_dot(mb, nb):
@@ -211,7 +252,7 @@
         @pl.loop(0, N_COL)
         def _(o):
             for q in range(MOST):
-                staged[nb, o, q] = rounded[tbl[O_BASE + o * MOST + q]]
+                staged[nb, o, q] = rounded[tbl[2 * SECTIONS, o * MOST + q]]
 
         where = out_ref.at[:, pl.ds(col * BC + nb * WIDE, WIDE)]
         for dy, dz in ORDER:
@@ -221,6 +262,7 @@
     stage_own(0)
     p_own(0)
     stage_own(1)
+    find()
     stage_near(0)
     stage_far(0)
     stage_second(0, 0)
@@ -273,40 +315,31 @@
         copy.wait()
 
 
-def tables(a_rows, a_cols, p_cols, owners):
-    codes = jnp.transpose(a_rows[0] * BK + a_cols[0], (1, 0, 2)).reshape(SECTIONS, A_SLOTS)
-    spots = jnp.arange(BR * BK, dtype=jnp.int32)
-    slots = jnp.arange(A_SLOTS, dtype=jnp.int32)
-    a_tbl = jnp.min(jnp.where(codes[:, None, :] == spots[None, :, None], slots[None, None, :], A_SLOTS), axis=2)
-    cols = jnp.transpose(p_cols[:, :, :, 0], (1, 0, 2, 3)).reshape(SECTIONS, P_SLOTS)
-    group = jnp.arange(BK * BC, dtype=jnp.int32)
-    slots = jnp.arange(P_SLOTS, dtype=jnp.int32)
-    place = (slots // PJ)[None, :] * BC + cols
-    p_tbl = jnp.min(jnp.where(place[:, None, :] == group[None, :, None], slots[None, None, :], P_SLOTS), axis=2)
-    owner = owners[:, 0]
-    line = jnp.arange(BR, dtype=jnp.int32)
-    rank = jnp.sum(((owner[:, None] == owner[None, :]) & (line[None, :] < line[:, None])).astype(jnp.int32), axis=1)
-    spot = owner * MOST + rank
-    outs = jnp.arange(N_COL * MOST, dtype=jnp.int32)
-    o_tbl = jnp.min(jnp.where(spot[None, :] == outs[:, None], line[None, :], BR), axis=1)
-    return jnp.concatenate([a_tbl.reshape(-1), p_tbl.reshape(-1), o_tbl]).astype(jnp.int32)
+def settle(held, out_ref, sems):
+    n = N_COL * BC // PIECES
+    copies = []
+    for q in range(MOST):
+        for i in range(PIECES):
+            part = (q, pl.ds(i * n, n))
+            copies.append(pltpu.make_async_copy(held.at[part], out_ref.at[part], sems.at[q * PIECES + i]))
+            copies[-1].start()
+    for copy in copies:
+        copy.wait()
 
 
 def body(a_tiles, a_rows, a_cols, p_tiles, p_cols, owners):
-    tbl = tables(a_rows, a_cols, p_cols, owners)
     a = a_tiles.reshape(SECTIONS, KA, TILE, TILE)
     p = p_tiles.reshape(SECTIONS, 2 * PJ, TILE, TILE)
     bf = jnp.bfloat16
-    return pl.pallas_call(
+    vmem = pl.BlockSpec(memory_space=pltpu.VMEM)
+    hbm = pl.BlockSpec(memory_space=pl.ANY)
+    shape = (MOST, N_COL * BC, TILE, TILE)
+    held = pl.pallas_call(
         kernel,
         name="block_product",
-        out_shape=jax.ShapeDtypeStruct((MOST, N_COL * BC, TILE, TILE), bf),
-        in_specs=[
-            pl.BlockSpec(memory_space=pltpu.SMEM),
-            pl.BlockSpec(memory_space=pl.ANY),
-            pl.BlockSpec(memory_space=pl.ANY),
-        ],
-        out_specs=pl.BlockSpec(memory_space=pl.ANY),
+        out_shape=pltpu.VMEM(shape, bf),
+        in_specs=[vmem] * 4 + [hbm] * 2,
+        out_specs=vmem,
         scratch_shapes=[pltpu.VMEM((A_SLOTS + 1, TILE, TILE), bf)] * SECTIONS
         + [pltpu.VMEM((P_SLOTS + 1, TILE, TILE), bf)] * SECTIONS
         + [
@@ -315,13 +348,32 @@
             pltpu.VMEM((CHUNKS, BR * TILE, WIDE * TILE), jnp.float32),
             pltpu.VMEM((BR + 1, WIDE, TILE, TILE), bf),
             pltpu.VMEM((CHUNKS, N_COL, MOST, WIDE, TILE, TILE), bf),
+            pltpu.VMEM((8, BR * BK), jnp.int32),
+            pltpu.SMEM((8, BR * BK), jnp.int32),
             pltpu.SemaphoreType.DMA((N_COPIES,)),
             pltpu.SemaphoreType.DMA((N_COPIES,)),
             pltpu.SemaphoreType.DMA((2 * SECTIONS + CHUNKS,)),
+            pltpu.SemaphoreType.DMA,
         ],
-        compiler_params=pltpu.CompilerParams(collective_id=0, has_side_effects=True, vmem_limit_bytes=60 << 20),
+        compiler_params=pltpu.CompilerParams(collective_id=0, has_side_effects=True, vmem_limit_bytes=52 << 20),
         cost_estimate=pl.CostEstimate(flops=25_769_803_776, bytes_accessed=20_000_000, transcendentals=0),
-    )(tbl, a, p)
+    )(
+        jnp.transpose(a_rows[0], (1, 2, 0)),
+        jnp.transpose(a_cols[0], (1, 2, 0)),
+        jnp.transpose(p_cols[:, :, :, 0], (1, 2, 3, 0)),
+        owners.reshape(1, BR),
+        a,
+        p,
+    )
+    return pl.pallas_call(
+        settle,
+        name="settle",
+        out_shape=jax.ShapeDtypeStruct(shape, bf),
+        in_specs=[vmem],
+        out_specs=hbm,
+        scratch_shapes=[pltpu.SemaphoreType.DMA((MOST * PIECES,))],
+        compiler_params=pltpu.CompilerParams(vmem_limit_bytes=2 << 20),
+    )(held)
 
 
 def solution(mesh):

time: 209 us -> 197 us (0.943)
  local copies, waits for them, and re-layouts: 11.6 us -> 0 us
  Pallas kernels: 193 us -> 197 us
  other arithmetic: 3.31 us -> 0 us
    unnamed x1 -> x0, local copies, waits for them, and re-layouts: 10.5 us -> none
    pallas_call x1 -> x2, Pallas kernels: 193 us -> 197 us  [the longest x1 193 us: body(): pl.pallas_call(kernel, name='block_product', out_shape=pltpu.VMEM(shape,...]
where the time goes in v2:
time: 197 us
  Pallas kernels  197 us (100%)
    pallas_call x1, Pallas kernels, body(): pl.pallas_call(kernel, name='block_product', out_shape=pltpu.VMEM(shape,...  193 us

profile of v2, /device:TPU:32, one launch (start us, length us, event | category | flops | bytes accessed | tf_op | source)
XLA Modules:
  0.0 196.6 jit_solution(17091211337908372198)
XLA Ops:
  0.0 193.2 %block_product.1.held = bf16[2,128,128,128]{3,2,1,0:T(8,128)(2,1)S(1)} custom-call(s32[3,8,16]{2,1,0:T(8,128)} %bitcast.14, s32[3,8,16]{2,1,0:T(8,128)} %bitcast.15, s32[3,2,4,8]{3,2,1,0:T(4,128)} %bitcast.16, s32[1,16]{1,0:T(1,128)} %bitcast.17, bf16[3,8,128,128]{3,2,1,0:T(8,128)(2,1)} %bitcast.12, bf16[3,8,128,128]{3,2,1,0:T(8,128)(2,1)} %bitcast.13), custom_call_target="tpu_custom_call" | custom-call | flops 25769803776 | bytes 20000000 | tf_op jit(solution)/shard_map/block_product/pallas_call | solution.py:337
  193.2 3.4 %settle.1 = bf16[2,128,128,128]{3,2,1,0:T(8,128)(2,1)} custom-call(bf16[2,128,128,128]{3,2,1,0:T(8,128)(2,1)S(1)} %block_product.1.held), custom_call_target="tpu_custom_call" | custom-call | tf_op jit(solution)/shard_map/settle/pallas_call | solution.py:368

commit v3 on v2

v3 whole, which is shorter than its diff:
```python
import functools

import jax
import jax.numpy as jnp
from jax import lax
from jax.experimental import pallas as pl
from jax.experimental.pallas import tpu as pltpu
from jax.sharding import PartitionSpec as P

SECTIONS = 3
BR = 16
BK = 16
BC = 8
KA = 8
PJ = 4
MOST = 2
TILE = 128
N_COL = 16
RING = 4
MESH = pl.DeviceIdType.MESH
A_SLOTS = N_COL * KA
P_SLOTS = BK * PJ
WIDE = 2
CHUNKS = BC // WIDE
MB = 1024
PIECES = 4

ORDER = (
    (0, 1), (1, 0), (2, 2), (0, 3), (3, 0), (1, 1), (3, 3), (2, 0),
    (0, 2), (1, 3), (3, 1), (1, 2), (2, 1), (3, 2), (2, 3),
)
RELAY = A_SLOTS + 1

HALF, QUARTER = KA // 2, KA // 4
SIDES = (1, 3)
PIECE = ((0, 0, HALF), (1, 0, HALF), (3, 0, HALF), (2, 0, QUARTER), (2, QUARTER, QUARTER))
KEYS = (
    [("by", n) for n in SIDES]
    + [("bf", n) for n in SIDES]
    + [("a_in",), ("a_cr",), ("a_cf",)]
    + [(kind, i) for kind in ("b_in", "b_cr", "b_cf") for i in range(len(PIECE))]
    + [(kind, j, n) for kind in ("ay", "af") for j in range(4) for n in SIDES]
    + [("share", dy) for dy in range(4)]
    + [("p_own",), ("p_cr", 0), ("p_cr", 1)]
    + [("px", j, n) for j in (0, 1) for n in SIDES]
    + [("pf", n) for n in SIDES]
)
IDS = {(s,) + key: s * len(KEYS) + i for s in range(SECTIONS) for i, key in enumerate(KEYS)}
TABLE_IDS = len(IDS)
OUT_IDS = TABLE_IDS + 2
N_COPIES = OUT_IDS + CHUNKS * N_COL


def kernel(
    a_rows, a_cols, p_cols, owners, a_ref, p_ref, out_ref,
    ar0, ar1, ar2, pr0, pr1, pr2, a_dense, p_dense, acc, rounded, staged, found, tbl, ssem, rsem, lsem, tsem,
):
    a_raw, p_raw = (ar0, ar1, ar2), (pr0, pr1, pr2)
    row, col = lax.axis_index("row"), lax.axis_index("col")
    x, core = row // 2, row % 2
    y, z = col // RING, col % RING
    half = z // 2
    inside = core == half
    pair = half * 2 + (z + 1) % 2
    cross = RING - 1 - z
    cz = jnp.where(inside, z, cross)
    work_row = x * 2 + half

    def when_in(f):
        pl.when(inside)(f)

    def when_out(f):
        pl.when(jnp.logical_not(inside))(f)

    def yz(dy, dz):
        return ((y + dy) % RING) * RING + (z + dz) % RING

    def at(dy, zz):
        return ((y + dy) % RING) * RING + zz

    def xrow(dx):
        return ((x + dx) % RING) * 2 + core

    sibling = x * 2 + 1 - core

    for s in range(SECTIONS):
        a_raw[s][A_SLOTS] = jnp.zeros((TILE, TILE), jnp.bfloat16)
        p_raw[s][P_SLOTS] = jnp.zeros((TILE, TILE), jnp.bfloat16)
    rounded[BR] = jnp.zeros((WIDE, TILE, TILE), jnp.bfloat16)

    barrier = pltpu.get_barrier_semaphore()
    peers = [{"col": yz(dy, dz)} for dy, dz in ORDER]
    peers += [{"row": sibling, "col": yz(dy, dz)} for dy, dz in ((0, 0),) + ORDER]
    peers += [{"row": xrow(dx)} for dx in SIDES]
    for peer in peers:
        pl.semaphore_signal(barrier, inc=1, device_id=peer, device_id_type=MESH)
    pl.semaphore_wait(barrier, len(peers))

    def remote(src, dst, peer, i, j=None):
        return pltpu.make_async_remote_copy(
            src_ref=src, dst_ref=dst, send_sem=ssem.at[i], recv_sem=rsem.at[i if j is None else j],
            device_id=peer, device_id_type=MESH,
        )

    def a_at(s, dy, zz, lo, n):
        return a_raw[s].at[pl.ds(at(dy, zz) * KA + lo, n)]

    def b_at(s, dy, lo, n):
        start = jnp.where(inside, at(dy, z) * KA + HALF, RELAY + ((y + dy) % RING) * HALF)
        return a_raw[s].at[pl.ds(start + lo, n)]

    def origin(j):
        return (z, pair, cross, RING - 1 - pair)[j]

    def p_at(s, xx, j):
        return p_raw[s].at[pl.ds((xx * 2 + j) * 2 * PJ, 2 * PJ)]

    def msg(s, *key):
        i = IDS[(s,) + key]
        kind = key[0]
        own = a_ref.at[s, pl.ds(HALF, HALF)]
        own_a = a_ref.at[s, pl.ds(0, HALF)]
        if kind == "by":
            return remote(own, b_at(s, 0, 0, HALF), {"col": yz(key[1], 0)}, i)
        if kind == "bf":
            part = b_at(s, -key[1], 0 if key[1] == 1 else QUARTER, QUARTER)
            return remote(part, part, {"col": yz(key[1], 0)}, i)
        if kind == "a_in":
            return remote(own_a, a_at(s, 0, z, 0, HALF), {"col": at(0, pair)}, i)
        if kind == "a_cr":
            return remote(own_a, a_at(s, 0, z, 0, HALF), {"col": at(0, cross)}, i)
        if kind == "a_cf":
            part = a_at(s, 0, cross, 0, HALF)
            return remote(part, part, {"col": at(0, pair)}, i)
        if kind in ("b_in", "b_cr"):
            dy, lo, n = PIECE[key[1]]
            src = own if dy == 0 else b_at(s, dy, lo, n)
            return remote(src, a_at(s, dy, z, HALF + lo, n), {"col": at(0, pair if kind == "b_in" else cross)}, i)
        if kind == "b_cf":
            dy, lo, n = PIECE[key[1]]
            part = a_at(s, dy, cross, HALF + lo, n)
            return remote(part, part, {"col": at(0, pair)}, i)
        if kind == "ay":
            part = a_at(s, 0, origin(key[1]), 0, HALF)
            return remote(own_a if key[1] == 0 else part, part, {"col": yz(key[2], 0)}, i)
        if kind == "af":
            part = a_at(s, -key[2], origin(key[1]), 0 if key[2] == 1 else QUARTER, QUARTER)
            return remote(part, part, {"col": yz(key[2], 0)}, i)
        if kind == "share":
            part = a_raw[s].at[pl.ds(at(key[1], 0) * KA, RING * KA)]
            return remote(part, part, {"row": sibling}, i)
        if kind == "p_own":
            return remote(p_ref.at[s], p_at(s, x, core), {"row": sibling}, i)
        if kind == "p_cr":
            mine = IDS[s, "p_cr", 0] + core
            return remote(p_ref.at[s], p_at(s, x, core), {"row": work_row, "col": at(0, cross)}, mine, mine if key[1] < 0 else i)
        if kind == "px":
            part = p_at(s, x, key[1])
            return remote(part, part, {"row": xrow(key[2])}, i)
        part = p_at(s, (x - key[1]) % RING, 0 if key[1] == 1 else 1)
        return remote(part, part, {"row": xrow(key[1])}, i)

    def start(s, *key):
        msg(s, *key).start()

    def wait(s, *key):
        msg(s, *key).wait_recv()

    def kept_a(s):
        return pltpu.make_async_copy(a_ref.at[s], a_at(s, 0, z, 0, KA), lsem.at[2 * s])

    def kept_p(s):
        return pltpu.make_async_copy(p_ref.at[s], p_at(s, x, core), lsem.at[2 * s + 1])

    def own(s):
        for n in SIDES:
            start(s, "by", n)

        @when_in
        def _():
            start(s, "a_in")
            for n in SIDES:
                start(s, "ay", 0, n)
            start(s, "b_in", 0)
            kept_a(s).start()

        @when_out
        def _():
            start(s, "a_cr")
            start(s, "b_cr", 0)

    def p_own(s):
        i = IDS[s, "p_cr", 0]
        cr = remote(p_ref.at[s], p_at(s, x, core), {"row": work_row, "col": at(0, cross)}, i + core, i + core)
        cr.start()

        @when_in
        def _():
            kept_p(s).start()

        @when_out
        def _():
            start(s, "p_own")

    def p_ring(s):
        for j in (0, 1):
            for n in SIDES:
                start(s, "px", j, n)

    def p_ring_in(s):
        @when_in
        def _():
            kept_p(s).wait()
            wait(s, "p_own")
            p_ring(s)

    def p_ring_out(s):
        @when_out
        def _():
            wait(s, "p_cr", 0)
            wait(s, "p_cr", 1)
            p_ring(s)

    def p_pass(s):
        wait(s, "px", 0, 1)
        start(s, "pf", 1)
        wait(s, "px", 1, 3)
        start(s, "pf", 3)

    def p_end(s):
        wait(s, "px", 1, 1)
        wait(s, "px", 0, 3)
        for n in SIDES:
            wait(s, "pf", n)

    def ring1(s):
        for n in SIDES:
            wait(s, "by", n)
            start(s, "bf", n)

        @when_in
        def _():
            start(s, "b_in", 2)
            start(s, "b_in", 1)

        @when_out
        def _():
            start(s, "b_cr", 2)
            start(s, "b_cr", 1)

    def ring2(s):
        for i, n in ((3, 1), (4, 3)):
            wait(s, "bf", n)

            @when_in
            def _():
                start(s, "b_in", i)

            @when_out
            def _():
                start(s, "b_cr", i)

    def alpha1(s):
        @when_in
        def _():
            wait(s, "a_cr")
            start(s, "a_cf")
            for n in SIDES:
                start(s, "ay", 2, n)
            wait(s, "a_in")
            for n in SIDES:
                start(s, "ay", 1, n)

    def alpha2(s):
        @when_in
        def _():
            wait(s, "a_cf")
            for n in SIDES:
                start(s, "ay", 3, n)

    def crossed(s, pieces):
        @when_in
        def _():
            for i in pieces:
                wait(s, "b_cr", i)
                start(s, "b_cf", i)

    def alpha3(s, origins):
        @when_in
        def _():
            for j in origins:
                for n in SIDES:
                    wait(s, "ay", j, n)
                    start(s, "af", j, n)

    def share(s, dy):
        @when_in
        def _():
            for i, (at_dy, _, _) in enumerate(PIECE):
                if at_dy == dy:
                    wait(s, "b_in", i)
                    wait(s, "b_cf", i)
            if dy == 0:
                kept_a(s).wait()
            if dy == 2:
                for j in range(4):
                    for n in SIDES:
                        wait(s, "af", j, n)
            start(s, "share", dy)

    def shared(s):
        @when_out
        def _():
            for dy in range(4):
                wait(s, "share", dy)

    def find():
        def iota(shape, dim):
            return lax.broadcasted_iota(jnp.int32, shape, dim)

        def column(line):
            n = line.shape[1]
            return jnp.sum(jnp.where(iota((n, n), 0) == iota((n, n), 1), line, 0), axis=1, keepdims=True)

        spots = iota((N_COL, BR * BK), 1)
        first = iota((N_COL, BR * BK), 0) * KA
        for s in range(SECTIONS):
            codes = a_rows[s] * BK + a_cols[s]
            best = jnp.full((N_COL, BR * BK), A_SLOTS, jnp.int32)
            for t in range(KA):
                best = jnp.minimum(best, jnp.where(column(codes[t : t + 1]) == spots, first + t, A_SLOTS))
            found[0, s : s + 1, :] = jnp.min(best, axis=0, keepdims=True)
        n_row = BK // 2
        spots = iota((n_row, BK * BC), 1)
        group = iota((n_row, BK * BC), 0)
        for s in range(SECTIONS):
            best = jnp.full((n_row, BK * BC), P_SLOTS, jnp.int32)
            for m in range(2):
                cols = p_cols[s, m]
                k = group * 2 + m
                for j in range(PJ):
                    best = jnp.minimum(best, jnp.where(k * BC + column(cols[j : j + 1]) == spots, k * PJ + j, P_SLOTS))
            found[1, s : s + 1, : BK * BC] = jnp.min(best, axis=0, keepdims=True)
        line = iota((BR, TILE), 0)
        spots = iota((BR, TILE), 1)
        named = column(owners[...]) == spots // MOST
        low = jnp.min(jnp.where(named, line, BR), axis=0, keepdims=True)
        high = jnp.max(jnp.where(named, line, -1), axis=0, keepdims=True)
        second = jnp.where(high > low, high, BR)
        slot = iota((1, TILE), 1) % MOST
        found[0, SECTIONS : SECTIONS + 1, :TILE] = jnp.where(slot == 0, low, second)

    def table_msgs():
        return (
            remote(found.at[0], found.at[0], {"row": sibling}, TABLE_IDS),
            remote(found.at[1], found.at[1], {"col": at(0, cross)}, TABLE_IDS + 1),
        )

    def find_tables():
        @when_in
        def _():
            find()
            for copy in table_msgs():
                copy.start()

    def take_tables():
        @when_out
        def _():
            for copy in table_msgs():
                copy.wait_recv()

        copy = pltpu.make_async_copy(found, tbl, tsem)
        copy.start()
        copy.wait()

    def place_p(s):
        @pl.loop(0, BK)
        def _(k):
            for c in range(BC):
                p_dense[pl.ds(pl.multiple_of(k * TILE, TILE), TILE), c * TILE : (c + 1) * TILE] = p_raw[s][
                    tbl[1, s, k * BC + c]
                ]

    def place_a(s):
        @pl.loop(0, BR)
        def _(r):
            for k in range(BK):
                a_dense[pl.ds(pl.multiple_of(r * TILE, TILE), TILE), k * TILE : (k + 1) * TILE] = a_raw[s][
                    tbl[0, s, r * BK + k]
                ]

    def part_dot(mb, nb):
        rows = pl.ds(pl.multiple_of(mb * MB, MB), MB)
        return jnp.dot(
            a_dense[rows, :], p_dense[:, nb * WIDE * TILE : (nb + 1) * WIDE * TILE], preferred_element_type=jnp.float32
        )

    def dots(s, nb):
        @pl.loop(0, BR * TILE // MB)
        def _(mb):
            rows = pl.ds(pl.multiple_of(mb * MB, MB), MB)
            value = part_dot(mb, nb)
            if s == 0:
                acc[nb, rows, :] = value
            else:
                acc[nb, rows, :] += value

    def finish(nb):
        @pl.loop(0, BR * TILE // MB)
        def _(mb):
            rows = pl.ds(pl.multiple_of(mb * MB, MB), MB)
            value = (acc[nb, rows, :] + part_dot(mb, nb)).astype(jnp.bfloat16)
            for i in range(MB // TILE):
                for j in range(WIDE):
                    rounded[mb * (MB // TILE) + i, j] = value[i * TILE : (i + 1) * TILE, j * TILE : (j + 1) * TILE]

        @pl.loop(0, N_COL)
        def _(o):
            for q in range(MOST):
                staged[nb, o, q] = rounded[tbl[0, SECTIONS, o * MOST + q]]

        @when_in
        def _():
            out_own(nb).start()

        @when_out
        def _():
            out_msg(nb, 0, 0).start()

        for dy, dz in ORDER:
            out_msg(nb, dy, dz).start()

    def out_at(nb, c):
        return out_ref.at[:, pl.ds(c * BC + nb * WIDE, WIDE)]

    def out_own(nb):
        return pltpu.make_async_copy(staged.at[nb, col], out_at(nb, col), lsem.at[2 * SECTIONS + nb])

    def out_msg(nb, dy, dz):
        base = OUT_IDS + nb * N_COL
        c = at(0, cz)
        o = yz(dy, dz)
        return remote(staged.at[nb, o], out_at(nb, c), {"row": work_row, "col": o}, base + o, base + c)

    def out_wait(nb):
        @pl.loop(0, N_COL)
        def _(c):
            @pl.when(jnp.logical_not(inside & (c == col)))
            def _():
                i = OUT_IDS + nb * N_COL + c
                remote(staged.at[nb, c], out_at(nb, c), {"row": sibling}, i, i).wait_recv()

    def sent():
        for s in range(SECTIONS):
            i = IDS[s, "p_cr", 0] + core
            remote(p_ref.at[s], p_at(s, x, core), {"row": work_row, "col": at(0, cross)}, i, i).wait_send()
            for key in KEYS:
                if key[0] in ("by", "bf", "px", "pf"):
                    msg(s, *key).wait_send()

        @when_in
        def _():
            for s in range(SECTIONS):
                for key in KEYS:
                    if key[0] in ("a_in", "a_cf", "b_in", "b_cf", "ay", "af", "share"):
                        msg(s, *key).wait_send()
            for copy in table_msgs():
                copy.wait_send()

        @when_out
        def _():
            for s in range(SECTIONS):
                for key in KEYS:
                    if key[0] in ("a_cr", "b_cr", "p_own"):
                        msg(s, *key).wait_send()

    def out_sent(nb):
        @when_in
        def _():
            out_own(nb).wait()

        @when_out
        def _():
            out_msg(nb, 0, 0).wait_send()

        for dy, dz in ORDER:
            out_msg(nb, dy, dz).wait_send()

    def moves(s):
        return [
            lambda: ring1(s),
            lambda: alpha1(s),
            lambda: p_ring_out(s),
            lambda: ring2(s),
            lambda: alpha2(s),
            lambda: crossed(s, (0, 1, 2)),
            lambda: p_pass(s),
            lambda: alpha3(s, (0,)),
            lambda: crossed(s, (3, 4)),
            lambda: alpha3(s, (2, 1)),
            lambda: share(s, 0),
            lambda: alpha3(s, (3,)),
            lambda: share(s, 1),
            lambda: share(s, 3),
            lambda: share(s, 2),
        ]

    def work(s):
        def first():
            p_end(s)
            place_p(s)
            shared(s)
            place_a(s)

        return [first] + [lambda nb=nb: dots(s, nb) for nb in range(1)]

    def mix(many, few):
        done = 0
        for i, f in enumerate(many):
            f()
            while done * len(many) < (i + 1) * len(few):
                few[done]()
                done += 1

    for step in plan(own, p_own, p_ring_in, find_tables, take_tables, moves, work):
        step()
    work(2)[0]()
    finish(0)
    for chunks in (range(1, 2), range(2, CHUNKS)):
        for s in range(SECTIONS):
            place_p(s)
            place_a(s)
            for nb in chunks:
                if s < SECTIONS - 1:
                    dots(s, nb)
                else:
                    finish(nb)
    sent()
    for nb in range(CHUNKS):
        out_sent(nb)
        out_wait(nb)


EARLY = 2
LAG = 3
TABLES = 8
AFTER = 15


def plan(own, p_own, p_ring_in, find_tables, take_tables, moves, work):
    steps = []
    for s in range(SECTIONS):
        if s < EARLY:
            steps += [functools.partial(own, s), functools.partial(p_own, s)]
        if s == 0:
            steps += [functools.partial(p_ring_in, 0)]
    timed = []
    for s in range(SECTIONS):
        for i, f in enumerate(moves(s)):
            timed.append((s * LAG + i, s, f))
        if s >= EARLY:
            timed.append((s * LAG - 3, s, functools.partial(own, s)))
            timed.append((s * LAG - 3, s, functools.partial(p_own, s)))
        if s:
            timed.append((s * LAG / 2 + 1 if s < EARLY else s * LAG - 2, s, functools.partial(p_ring_in, s)))
    timed.append((TABLES, 0, find_tables))
    timed.append((AFTER, 0, take_tables))
    for s in range(SECTIONS - 1):
        for i, f in enumerate(work(s)):
            timed.append((s * LAG + AFTER + i, 9, f))
    timed.sort(key=lambda t: t[:2])
    return steps + [f for _, _, f in timed]


def settle(held, out_ref, sems):
    n = N_COL * BC // PIECES
    copies = []
    for q in range(MOST):
        for i in range(PIECES):
            part = (q, pl.ds(i * n, n))
            copies.append(pltpu.make_async_copy(held.at[part], out_ref.at[part], sems.at[q * PIECES + i]))
            copies[-1].start()
    for copy in copies:
        copy.wait()


def body(a_tiles, a_rows, a_cols, p_tiles, p_cols, owners):
    a = a_tiles.reshape(SECTIONS, KA, TILE, TILE)
    p = p_tiles.reshape(SECTIONS, 2 * PJ, TILE, TILE)
    bf = jnp.bfloat16
    vmem = pl.BlockSpec(memory_space=pltpu.VMEM)
    hbm = pl.BlockSpec(memory_space=pl.ANY)
    shape = (MOST, N_COL * BC, TILE, TILE)
    held = pl.pallas_call(
        kernel,
        name="block_product",
        out_shape=pltpu.VMEM(shape, bf),
        in_specs=[vmem] * 4 + [hbm] * 2,
        out_specs=vmem,
        scratch_shapes=[pltpu.VMEM((RELAY + RING * HALF, TILE, TILE), bf)] * SECTIONS
        + [pltpu.VMEM((P_SLOTS + 1, TILE, TILE), bf)] * SECTIONS
        + [
            pltpu.VMEM((BR * TILE, BK * TILE), bf),
            pltpu.VMEM((BK * TILE, BC * TILE), bf),
            pltpu.VMEM((CHUNKS, BR * TILE, WIDE * TILE), jnp.float32),
            pltpu.VMEM((BR + 1, WIDE, TILE, TILE), bf),
            pltpu.VMEM((CHUNKS, N_COL, MOST, WIDE, TILE, TILE), bf),
            pltpu.VMEM((2, 8, BR * BK), jnp.int32),
            pltpu.SMEM((2, 8, BR * BK), jnp.int32),
            pltpu.SemaphoreType.DMA((N_COPIES,)),
            pltpu.SemaphoreType.DMA((N_COPIES,)),
            pltpu.SemaphoreType.DMA((2 * SECTIONS + CHUNKS,)),
            pltpu.SemaphoreType.DMA,
        ],
        compiler_params=pltpu.CompilerParams(collective_id=0, has_side_effects=True, vmem_limit_bytes=52 << 20),
        cost_estimate=pl.CostEstimate(flops=25_769_803_776, bytes_accessed=20_000_000, transcendentals=0),
    )(
        jnp.transpose(a_rows[0], (1, 2, 0)),
        jnp.transpose(a_cols[0], (1, 2, 0)),
        jnp.transpose(p_cols[:, :, :, 0], (1, 2, 3, 0)),
        owners.reshape(1, BR),
        a,
        p,
    )
    return pl.pallas_call(
        settle,
        name="settle",
        out_shape=jax.ShapeDtypeStruct(shape, bf),
        in_specs=[vmem],
        out_specs=hbm,
        scratch_shapes=[pltpu.SemaphoreType.DMA((MOST * PIECES,))],
        compiler_params=pltpu.CompilerParams(vmem_limit_bytes=2 << 20),
    )(held)


def solution(mesh):
    placed = (
        P("row", "col", None, None, None, None),
        P("row", None, None, None),
        P("row", None, None, None),
        P("row", None, None, "col", None, None, None),
        P(None, None, None, "col", None),
        P("row", None),
    )
    return jax.shard_map(
        body,
        mesh=mesh,
        in_specs=placed,
        out_specs=P(("row", "col"), None, None, None),
        check_vma=False,
    )
```

time: 197 us -> 175 us (0.89)
  Pallas kernels: 197 us -> 173 us
    pallas_call x1, Pallas kernels: 193 us -> 170 us  [body(): pl.pallas_call(kernel, name='block_product', out_shape=pltpu.VMEM(shape,...]
where the time goes in v3:
time: 175 us; the launch traced here: 173 us
  Pallas kernels  173 us (99%)
    pallas_call x1, Pallas kernels, body(): pl.pallas_call(kernel, name='block_product', out_shape=pltpu.VMEM(shape,...  170 us

profile of v3, /device:TPU:32, one launch (start us, length us, event | category | flops | bytes accessed | tf_op | source)
XLA Modules:
  0.0 173.4 jit_solution(11470222613460027439)
XLA Ops:
  0.0 169.9 %block_product.1.held = bf16[2,128,128,128]{3,2,1,0:T(8,128)(2,1)S(1)} custom-call(s32[3,8,16]{2,1,0:T(8,128)} %bitcast.14, s32[3,8,16]{2,1,0:T(8,128)} %bitcast.15, s32[3,2,4,8]{3,2,1,0:T(4,128)} %bitcast.16, s32[1,16]{1,0:T(1,128)} %bitcast.17, bf16[3,8,128,128]{3,2,1,0:T(8,128)(2,1)} %bitcast.12, bf16[3,8,128,128]{3,2,1,0:T(8,128)(2,1)} %bitcast.13), custom_call_target="tpu_custom_call" | custom-call | flops 25769803776 | bytes 20000000 | tf_op jit(solution)/shard_map/block_product/pallas_call | solution.py:594
  169.9 3.4 %settle.1 = bf16[2,128,128,128]{3,2,1,0:T(8,128)(2,1)} custom-call(bf16[2,128,128,128]{3,2,1,0:T(8,128)(2,1)S(1)} %block_product.1.held), custom_call_target="tpu_custom_call" | custom-call | tf_op jit(solution)/shard_map/settle/pallas_call | solution.py:625

commit v4 on v3

--- a/solution.py
+++ b/solution.py
@@ -48,6 +48,7 @@
 IDS = {(s,) + key: s * len(KEYS) + i for s in range(SECTIONS) for i, key in enumerate(KEYS)}
 TABLE_IDS = len(IDS)
 OUT_IDS = TABLE_IDS + 2
+TURN = 4
 N_COPIES = OUT_IDS + CHUNKS * N_COL
 
 
@@ -427,7 +428,7 @@
         def _():
             out_msg(nb, 0, 0).start()
 
-        for dy, dz in ORDER:
+        for dy, dz in out_order():
             out_msg(nb, dy, dz).start()
 
     def out_at(nb, c):
@@ -473,6 +474,10 @@
                 for key in KEYS:
                     if key[0] in ("a_cr", "b_cr", "p_own"):
                         msg(s, *key).wait_send()
+
+    def out_order():
+        for (dy, dz), (oy, oz) in zip(ORDER, ORDER[TURN:] + ORDER[:TURN]):
+            yield jnp.where(inside, dy, oy), jnp.where(inside, dz, oz)
 
     def out_sent(nb):
         @when_in

time: 175 us -> 174 us (level)
  the two profiles are of different devices: /device:TPU:32 before, /device:TPU:92 now
where the time goes in v4:
time: 174 us
  Pallas kernels  174 us (100%)
    pallas_call x1, Pallas kernels, body(): pl.pallas_call(kernel, name='block_product', out_shape=pltpu.VMEM(shape,...  170 us

profile of v4, /device:TPU:92, one launch (start us, length us, event | category | flops | bytes accessed | tf_op | source)
XLA Modules:
  0.0 173.8 jit_solution(6185888278893662635)
XLA Ops:
  0.0 170.2 %block_product.1.held = bf16[2,128,128,128]{3,2,1,0:T(8,128)(2,1)S(1)} custom-call(s32[3,8,16]{2,1,0:T(8,128)} %bitcast.14, s32[3,8,16]{2,1,0:T(8,128)} %bitcast.15, s32[3,2,4,8]{3,2,1,0:T(4,128)} %bitcast.16, s32[1,16]{1,0:T(1,128)} %bitcast.17, bf16[3,8,128,128]{3,2,1,0:T(8,128)(2,1)} %bitcast.12, bf16[3,8,128,128]{3,2,1,0:T(8,128)(2,1)} %bitcast.13), custom_call_target="tpu_custom_call" | custom-call | flops 25769803776 | bytes 20000000 | tf_op jit(solution)/shard_map/block_product/pallas_call | solution.py:599
  170.2 3.4 %settle.1 = bf16[2,128,128,128]{3,2,1,0:T(8,128)(2,1)} custom-call(bf16[2,128,128,128]{3,2,1,0:T(8,128)(2,1)S(1)} %block_product.1.held), custom_call_target="tpu_custom_call" | custom-call | tf_op jit(solution)/shard_map/settle/pallas_call | solution.py:630

commit v5 on v4

--- a/solution.py
+++ b/solution.py
@@ -47,14 +47,14 @@
 )
 IDS = {(s,) + key: s * len(KEYS) + i for s in range(SECTIONS) for i, key in enumerate(KEYS)}
 TABLE_IDS = len(IDS)
-OUT_IDS = TABLE_IDS + 2
+OUT_IDS = TABLE_IDS + 3
 TURN = 4
 N_COPIES = OUT_IDS + CHUNKS * N_COL
 
 
 def kernel(
     a_rows, a_cols, p_cols, owners, a_ref, p_ref, out_ref,
-    ar0, ar1, ar2, pr0, pr1, pr2, a_dense, p_dense, acc, rounded, staged, found, tbl, ssem, rsem, lsem, tsem,
+    ar0, ar1, ar2, pr0, pr1, pr2, a_dense, p_dense, acc, rounded, staged, found, taken, tbl, ssem, rsem, lsem, tsem,
 ):
     a_raw, p_raw = (ar0, ar1, ar2), (pr0, pr1, pr2)
     row, col = lax.axis_index("row"), lax.axis_index("col")
@@ -353,24 +353,29 @@
 
     def table_msgs():
         return (
-            remote(found.at[0], found.at[0], {"row": sibling}, TABLE_IDS),
-            remote(found.at[1], found.at[1], {"col": at(0, cross)}, TABLE_IDS + 1),
+            remote(found.at[0], taken.at[0], {"col": at(0, cross)}, TABLE_IDS),
+            remote(found.at[1], taken.at[1], {"row": sibling}, TABLE_IDS + 1),
+            remote(found, taken, {"row": sibling, "col": at(0, cross)}, TABLE_IDS + 2),
         )
 
     def find_tables():
-        @when_in
+        @when_out
         def _():
             find()
             for copy in table_msgs():
                 copy.start()
 
     def take_tables():
-        @when_out
-        def _():
-            for copy in table_msgs():
+        @when_in
+        def _():
+            for copy in table_msgs()[:2]:
                 copy.wait_recv()
 
-        copy = pltpu.make_async_copy(found, tbl, tsem)
+        @when_out
+        def _():
+            table_msgs()[2].wait_recv()
+
+        copy = pltpu.make_async_copy(taken, tbl, tsem)
         copy.start()
         copy.wait()
 
@@ -465,8 +470,6 @@
                 for key in KEYS:
                     if key[0] in ("a_in", "a_cf", "b_in", "b_cf", "ay", "af", "share"):
                         msg(s, *key).wait_send()
-            for copy in table_msgs():
-                copy.wait_send()
 
         @when_out
         def _():
@@ -474,6 +477,8 @@
                 for key in KEYS:
                     if key[0] in ("a_cr", "b_cr", "p_own"):
                         msg(s, *key).wait_send()
+            for copy in table_msgs():
+                copy.wait_send()
 
     def out_order():
         for (dy, dz), (oy, oz) in zip(ORDER, ORDER[TURN:] + ORDER[:TURN]):
@@ -610,6 +615,7 @@
             pltpu.VMEM((CHUNKS, BR * TILE, WIDE * TILE), jnp.float32),
             pltpu.VMEM((BR + 1, WIDE, TILE, TILE), bf),
             pltpu.VMEM((CHUNKS, N_COL, MOST, WIDE, TILE, TILE), bf),
+            pltpu.VMEM((2, 8, BR * BK), jnp.int32),
             pltpu.VMEM((2, 8, BR * BK), jnp.int32),
             pltpu.SMEM((2, 8, BR * BK), jnp.int32),
             pltpu.SemaphoreType.DMA((N_COPIES,)),

time: 174 us -> 174 us (level)
  no operation moved by 1% of the time
where the time goes in v5:
time: 174 us
  Pallas kernels  174 us (100%)
    pallas_call x1, Pallas kernels, body(): pl.pallas_call(kernel, name='block_product', out_shape=pltpu.VMEM(shape,...  170 us

profile of v5, /device:TPU:92, one launch (start us, length us, event | category | flops | bytes accessed | tf_op | source)
XLA Modules:
  0.0 173.9 jit_solution(6233344482393628297)
XLA Ops:
  0.0 170.4 %block_product.1.held = bf16[2,128,128,128]{3,2,1,0:T(8,128)(2,1)S(1)} custom-call(s32[3,8,16]{2,1,0:T(8,128)} %bitcast.14, s32[3,8,16]{2,1,0:T(8,128)} %bitcast.15, s32[3,2,4,8]{3,2,1,0:T(4,128)} %bitcast.16, s32[1,16]{1,0:T(1,128)} %bitcast.17, bf16[3,8,128,128]{3,2,1,0:T(8,128)(2,1)} %bitcast.12, bf16[3,8,128,128]{3,2,1,0:T(8,128)(2,1)} %bitcast.13), custom_call_target="tpu_custom_call" | custom-call | flops 25769803776 | bytes 20000000 | tf_op jit(solution)/shard_map/block_product/pallas_call | solution.py:604
  170.4 3.4 %settle.1 = bf16[2,128,128,128]{3,2,1,0:T(8,128)(2,1)} custom-call(bf16[2,128,128,128]{3,2,1,0:T(8,128)(2,1)S(1)} %block_product.1.held), custom_call_target="tpu_custom_call" | custom-call | tf_op jit(solution)/shard_map/settle/pallas_call | solution.py:636
